TPU v7x, 512 devices: a whole 4x4x16 slice. The times are simulated.
512 devices in a mesh: sec: 32 (over y, x, core), env: 16 (over z).
Axes of the slice: x: 4, y: 4, z: 16, core: 2. Of those that a mesh axis runs over, the one named last changes fastest.
Arguments:
- wavefunction: float32 [32, 512, 512], P('sec', 'env'), may hold values from -14 to 14
- left_env: bfloat16 [34, 512, 512], P(None, 'env'), may hold values from -0.176776695 to 0.176776695
- right_env: bfloat16 [34, 512, 512], P(None, 'env'), may hold values from -0.25 to 0.25
- task_in: int32 [512], replicated, may hold values from 0 to 31
- task_out: int32 [512, 1], replicated, may hold values from 0 to 31; in each aligned block of 512 rows (0 to 511, 512 to 1023, ...) at most 64 rows name the same one
- task_term: int32 [512], replicated, may hold values from 0 to 33
Outputs:
- sigma: float32 [32, 512, 512], P('sec', 'env')
Inputs may be any that keep to these rules, and one draw needn't show every extreme that they name: `task_out`: no sector is the target of more than 64 tasks, and in every draw some sector is the target of exactly 64.
All inputs are finite; a program needn't handle non-finite values.
Results may differ from a plain program's by a relative error of at most 0.00045.
Values may be sent and summed in bfloat16 or wider, within the bound.
A program may use at most 64 MiB of HBM per device.

v0:
```python
import jax
import jax.numpy as jnp
from jax import lax
from jax.sharding import PartitionSpec as P


def laid_out(pieces, dim):
    pieces = jnp.moveaxis(pieces, 0, dim)
    dims = pieces.shape
    return pieces.reshape(*dims[:dim], dims[dim] * dims[dim + 1], *dims[dim + 2 :])


def from_everyone(array, axis):
    copies = jnp.broadcast_to(array, (lax.axis_size(axis), *array.shape))
    return lax.all_to_all(copies, axis, split_axis=0, concat_axis=0, tiled=True)


def collect(array, axis, dim):
    return laid_out(from_everyone(array, axis), dim)


def sent_together(arrays, axis, split_dim, concat_dim, along):
    widths = [a.shape[along] for a in arrays]
    both = jnp.concatenate(arrays, axis=along)
    filled = lax.all_to_all(both, axis, split_axis=split_dim, concat_axis=concat_dim, tiled=True)
    return tuple(jnp.split(filled, [sum(widths[:k]) for k in range(1, len(widths))], axis=along))


def cut_along(array, dim, peers):
    before, after = (array.shape[:dim], array.shape[dim + 1 :])
    return jnp.moveaxis(array.reshape(*before, peers, -1, *after), dim, 0)


def sent_and_summed(array, axis, dim):
    pieces = cut_along(array, dim, lax.axis_size(axis))
    arrived = lax.all_to_all(pieces, axis, split_axis=0, concat_axis=0, tiled=True)
    return arrived.sum(axis=0)


def pick_values(values, task_ids):
    hits = task_ids[:, None] == jnp.arange(values.shape[0], dtype=jnp.int32)[None, :]
    return jnp.sum(jnp.where(hits, values[None, :], 0), axis=1)


def task_product(high_block, low_block, left_block, right_block):
    mixed_sum = jnp.dot(high_block, right_block, preferred_element_type=jnp.float32) + jnp.dot(
        low_block, right_block, preferred_element_type=jnp.float32
    )
    top_part = lax.optimization_barrier(mixed_sum.astype(jnp.bfloat16))
    rest_part = (mixed_sum - top_part.astype(jnp.float32)).astype(jnp.bfloat16)
    return jnp.dot(left_block, top_part, preferred_element_type=jnp.float32) + jnp.dot(
        left_block, rest_part, preferred_element_type=jnp.float32
    )


def body(wavefunction, left_env, right_env, task_in, task_out, task_term):
    row_count = wavefunction.shape[1]
    col_count = wavefunction.shape[2]
    groups = lax.axis_size("sec")
    env_count = lax.axis_size("env")
    my_group = lax.axis_index("sec")
    task_count = task_in.shape[0]
    per_device = task_count // (groups * env_count)
    all_rows = collect(wavefunction, "sec", 0)
    high_rows = lax.optimization_barrier(all_rows.astype(jnp.bfloat16))
    low_rows = (all_rows - high_rows.astype(jnp.float32)).astype(jnp.bfloat16)
    targets = task_out[:, 0]

    def outgoing(peer_tasks):
        sources = pick_values(task_in, peer_tasks)
        term_ids = pick_values(task_term, peer_tasks)
        high_send = jnp.take(high_rows, sources, axis=0)
        low_send = jnp.take(low_rows, sources, axis=0)
        left_send = jnp.take(left_env, term_ids, axis=0)
        right_send = jnp.take(right_env, term_ids, axis=0)
        return (high_send, low_send, left_send, right_send)

    first_task = my_group * per_device * env_count

    def even_slot(slot_id, buffer):
        peer_tasks = first_task + slot_id * env_count + jnp.arange(env_count, dtype=jnp.int32)
        high_send, low_send, left_send, right_send = outgoing(peer_tasks)
        high_block, low_block, left_block, right_block = sent_together(
            (high_send, low_send, left_send, right_send), "env", 0, 1, 2
        )
        own_partial = task_product(high_block[0], low_block[0], left_block[0], right_block[0])
        split_rows = own_partial.reshape(env_count, row_count, col_count)
        received = lax.all_to_all(split_rows, "env", split_axis=0, concat_axis=0, tiled=True)
        peer_targets = pick_values(targets, peer_tasks)
        target_hits = (
            jnp.arange(groups, dtype=jnp.int32)[:, None] == peer_targets[None, :]
        ).astype(jnp.float32)
        return buffer + jnp.einsum(
            "gk,krc->grc", target_hits, received, precision=lax.Precision.HIGHEST
        )

    buffer = lax.fori_loop(
        0, per_device, even_slot, jnp.zeros((groups, row_count, col_count), jnp.float32)
    )
    return sent_and_summed(buffer, "sec", 0)


def solution(mesh):
    placed = (P("sec", "env", None), P(None, "env", None), P(None, "env", None), P(), P(), P())
    return jax.shard_map(
        body, mesh=mesh, in_specs=placed, out_specs=P("sec", "env", None), check_vma=False
    )
```

profile of v0, /device:TPU:1, one launch (start us, length us, event | category | flops | bytes accessed | tf_op | source)
XLA Modules:
  0.0 258.0 jit_solution(2485152752231201467)
XLA Ops:
  0.0 0.0 copy-start
  0.0 2.5 broadcast_in_dim.77
  2.6 10.7 %all-to-all-start = ((f32[32,1,32,512]{3,2,1,0:T(8,128)}), f32[32,1,32,512]{3,2,1,0:T(8,128)S(1)}, u32[]{:S(2)}, u32[]{:S(2)}) async-start(f32[32,1,32,512]{3,2,1,0:T(8,128)} %broadcast_in_dim.77), calls=%async_computation | async-start | bytes 4194304 | tf_op jit(solution)/shard_map/all_to_all | solution.py:15
  13.2 0.0 copy-done.1
  13.3 0.2 select_reduce_fusion.2
  13.5 1.4 gather_fusion.2
  14.9 2.6 %gather_fusion.3 = bf16[16,32,512]{2,1,0:T(8,128)(2,1)} fusion(bf16[34,32,512]{2,1,0:T(8,128)(2,1)} %param.12, s32[1024]{0:T(1024)S(1)} %pad_clamp_fusion), kind=kCustom, calls=%fused_computation.3.clone | custom fusion | bytes 1048640 | tf_op jit(solution)/shard_map/while/body/eval_jaxpr/jit(_take)/gather | solution.py:75
  17.6 23.6 %all-to-all-done = f32[32,1,32,512]{3,2,1,0:T(8,128)S(1)} async-done(((f32[32,1,32,512]{3,2,1,0:T(8,128)}), f32[32,1,32,512]{3,2,1,0:T(8,128)S(1)}, u32[]{:S(2)}, u32[]{:S(2)}) %all-to-all-start) | async-done | bytes 2097184 | tf_op jit(solution)/shard_map/all_to_all | solution.py:15
  41.2 1.2 bitcast_convert_fusion
  42.3 2.6 %gather_fusion = bf16[16,32,512]{2,1,0:T(8,128)(2,1)} fusion(bf16[32,32,512]{2,1,0:T(8,128)(2,1)} %bitcast_convert_fusion, s32[1024]{0:T(1024)S(1)} %pad_clamp_fusion.1), kind=kCustom, calls=%fused_computation.clone | custom fusion | bytes 1048640 | tf_op jit(solution)/shard_map/while/body/eval_jaxpr/jit(_take)/gather | solution.py:72
  45.0 2.6 %fusion = bf16[32,32,512]{2,1,0:T(8,128)(2,1)} fusion(f32[32,1,32,512]{3,2,1,0:T(8,128)S(1)} %all-to-all-done, bf16[32,32,512]{2,1,0:T(8,128)(2,1)} %bitcast_convert_fusion), kind=kLoop, calls=%fused_computation.7 | loop fusion | flops 1572864 | bytes 4194304 | tf_op jit(solution)/shard_map/convert_element_type | solution.py:66
  47.6 1.8 gather_fusion.1
  49.4 1.6 broadcast_select_fusion.1
  51.0 0.3 pad_maximum_fusion
  51.3 101.6 %all_to_all.32 = bf16[16,32,2048]{2,1,0:T(8,128)(2,1)S(1)} all-to-all(bf16[16,32,2048]{2,1,0:T(8,128)(2,1)S(1)} %pad_maximum_fusion), channel_id=1, replica_groups=mesh['sec'=32,'env'=16] {'env'}, dimensions={0} | all-to-all | bytes 4194304 | tf_op jit(solution)/shard_map/while/body/eval_jaxpr/all_to_all | solution.py:25
  152.9 0.4 fusion.2
  153.3 0.4 fusion.7
  153.8 0.4 fusion.3
  154.2 0.5 convolution_add_fusion
  154.7 57.1 %all_to_all.33 = f32[16,32,512]{2,1,0:T(8,128)S(1)} all-to-all(f32[16,32,512]{2,1,0:T(8,128)S(1)} %bitcast.38), channel_id=1, replica_groups=mesh['sec'=32,'env'=16] {'env'}, dimensions={0} | all-to-all | bytes 2097152 | tf_op jit(solution)/shard_map/while/body/eval_jaxpr/all_to_all | solution.py:88
  211.7 1.6 convolution_bitcast_fusion
  213.3 1.2 copy.11
  214.6 42.7 %all_to_all.34 = f32[32,1,32,512]{3,2,1,0:T(8,128)S(1)} all-to-all(f32[32,1,32,512]{3,2,1,0:T(8,128)S(1)} %copy.11), channel_id=1, replica_groups=mesh['sec'=32,'env'=16] {'sec'}, dimensions={0} | all-to-all | bytes 4194304 | tf_op jit(solution)/shard_map/all_to_all | solution.py:36
  257.2 0.8 reduce_sum.44
  (13 shorter events, 0.1 us)
Async XLA Ops:
  0.0 13.5 %copy-start = (bf16[34,32,512]{2,1,0:T(8,128)(2,1)S(1)}, bf16[34,32,512]{2,1,0:T(8,128)(2,1)}, u32[]{:S(2)}) copy-start(bf16[34,32,512]{2,1,0:T(8,128)(2,1)} %param.11) | copy-start | bytes 3342340
  2.5 10.7 %copy-start.1 = (s32[512,1]{0,1:T(1,128)S(1)}, s32[512,1]{0,1:T(1,128)}, u32[]{:S(2)}) copy-start(s32[512,1]{0,1:T(1,128)} %param.14) | copy-start | bytes 6148
  2.5 10.7 %copy-start.2 = (s32[512]{0:T(512)S(1)}, s32[512]{0:T(512)}, u32[]{:S(2)}) copy-start(s32[512]{0:T(512)} %param.15) | copy-start | bytes 6148
  2.6 10.7 %copy-start.3 = (s32[512]{0:T(512)S(1)}, s32[512]{0:T(512)}, u32[]{:S(2)}) copy-start(s32[512]{0:T(512)} %param.13) | copy-start | bytes 6148
  2.6 38.6 %all-to-all-start = ((f32[32,1,32,512]{3,2,1,0:T(8,128)}), f32[32,1,32,512]{3,2,1,0:T(8,128)S(1)}, u32[]{:S(2)}, u32[]{:S(2)}) async-start(f32[32,1,32,512]{3,2,1,0:T(8,128)} %broadcast_in_dim.77), calls=%async_computation | async-start | bytes 4194304 | tf_op jit(solution)/shard_map/all_to_all | solution.py:15
where the time goes:
time: 259 us; the launch traced here: 258 us
  blocking collectives  201 us (78%)
  waiting for transfers between devices  23.6 us (9%)
  local copies, waits for them, and re-layouts  12.2 us (5%)
  starting transfers between devices  10.7 us (4%)
  other arithmetic  6.69 us (3%)
  matrix products  3.35 us (1%)
    all_to_all x1, blocking collectives, sent_together(): lax.all_to_all(both, axis, split_axis=split_dim, concat_axis=concat_dim,...  102 us
    all_to_all x1, blocking collectives, even_slot(): lax.all_to_all(split_rows, 'env', split_axis=0, concat_axis=0, tiled=True)  57.1 us
    all_to_all x1, blocking collectives, sent_and_summed(): lax.all_to_all(pieces, axis, split_axis=0, concat_axis=0, tiled=True)  42.7 us
    all_to_all x1, waiting for transfers between devices, from_everyone(): return lax.all_to_all(copies, axis, split_axis=0, concat_axis=0, tiled=True)  23.6 us
    all_to_all x1, starting transfers between devices, from_everyone(): return lax.all_to_all(copies, axis, split_axis=0, concat_axis=0, tiled=True)  10.7 us
  transfers between devices with their start and end apart: 1, of which 1 were waited for; matrix products, arithmetic and copies ran while one was open for 2% of the time, Pallas kernels for 0%

commit v1 on v0

v1 whole, which is shorter than its diff:
```python
import functools

import jax
import jax.numpy as jnp
from jax import lax
from jax.experimental import pallas as pl
from jax.experimental.pallas import tpu as pltpu
from jax.sharding import PartitionSpec as P

MESH = pl.DeviceIdType.MESH
F32 = jnp.float32
BF16 = jnp.bfloat16


def vmem():
    return pl.BlockSpec(memory_space=pltpu.VMEM)


def gather_kernel(groups, ring, psi_ref, left_ref, right_ref, q_ref, rt_ref, t_scr, send_buf, got, hl, rg, rrow,
                  a_send, a_recv, z_send, z_recv):
    g = lax.axis_index("sec")
    e = lax.axis_index("env")
    terms = left_ref.shape[0]
    rows = psi_ref.shape[1]
    cols = psi_ref.shape[2]
    per = cols // groups
    right = lax.rem(e + 1, ring)
    left = lax.rem(e + ring - 1, ring)

    barrier = pltpu.get_barrier_semaphore()
    for d in range(1, groups):
        pl.semaphore_signal(barrier, inc=1, device_id={"sec": lax.rem(g + d, groups)}, device_id_type=MESH)
    for to in (left, right):
        pl.semaphore_signal(barrier, inc=1, device_id={"env": to}, device_id_type=MESH)

    psi = psi_ref[0]
    high = psi.astype(BF16)
    low = (psi - high.astype(F32)).astype(BF16)
    stacked = jnp.concatenate(
        [high.astype(F32), low.astype(F32), jnp.zeros((128 - 2 * rows, cols), F32)], axis=0
    )
    t_scr[...] = stacked.T
    for p in range(groups):
        send_buf[p] = t_scr[pl.ds(p, per, stride=groups), :].astype(BF16)

    pl.semaphore_wait(barrier, groups + 1)

    spread = []
    for d in range(1, groups):
        to = lax.rem(g + d, groups)
        copy = pltpu.make_async_remote_copy(
            src_ref=send_buf.at[to],
            dst_ref=got.at[g],
            send_sem=a_send.at[d],
            recv_sem=a_recv.at[d],
            device_id={"sec": to},
            device_id_type=MESH,
        )
        copy.start()
        spread.append(copy)
    got[g] = send_buf[g]

    rrow[...] = jnp.zeros_like(rrow)
    pick = lax.broadcasted_iota(jnp.int32, (rows, cols), 0) == g
    for w in range(terms):
        row = jnp.sum(jnp.where(pick, right_ref[w].astype(F32), 0.0), axis=0, keepdims=True)
        rrow[pl.ds(w, 1), :] = row
    rg[e] = rrow[...].astype(BF16)

    for copy in spread:
        copy.wait_recv()
    back = got[...].astype(F32).reshape(groups * per, 128).T
    hl[e] = back[: 2 * rows].astype(BF16)

    def z_copy(buffer, slot, to, index):
        return pltpu.make_async_remote_copy(
            src_ref=buffer.at[slot],
            dst_ref=buffer.at[slot],
            send_sem=z_send.at[index],
            recv_sem=z_recv.at[index],
            device_id={"env": to},
            device_id_type=MESH,
        )

    ways = ((right, -1, ring // 2), (left, 1, ring // 2 - 1))
    flights = {}
    for h in range(ring // 2):
        for b, buffer in enumerate((hl, rg)):
            for way, (to, sign, hops) in enumerate(ways):
                if h > 0 and (way, b, h - 1) in flights:
                    flights[way, b, h - 1].wait_recv()
                if h < hops:
                    slot = lax.rem(e + sign * h + ring, ring)
                    copy = z_copy(buffer, slot, to, (b * 2 + way) * (ring // 2) + h)
                    copy.start()
                    flights[way, b, h] = copy
    for b in range(2):
        flights[0, b, ring // 2 - 1].wait_recv()

    block = cols // 2
    lanes = q_ref.shape[3]
    lhs = left_ref[...].reshape(terms * rows, cols)
    for half in range(2):
        x_high = hl[:, :rows, half * block : (half + 1) * block].reshape(ring * rows, block)
        x_low = hl[:, rows:, half * block : (half + 1) * block].reshape(ring * rows, block)
        q = jnp.dot(lhs, x_high, preferred_element_type=F32) + jnp.dot(lhs, x_low, preferred_element_type=F32)
        for part in range(block // lanes):
            q_ref[:, half * (block // lanes) + part] = q[:, part * lanes : (part + 1) * lanes].reshape(
                terms, rows, lanes
            )

    padded = rg.shape[1]
    out_row = lax.broadcasted_iota(jnp.int32, (rt_ref.shape[0], ring * padded), 0)
    in_row = lax.broadcasted_iota(jnp.int32, (rt_ref.shape[0], ring * padded), 1)
    same = (out_row // ring == in_row % padded) & (out_row % ring == in_row // padded) & (out_row < terms * ring)
    order = jnp.where(same, 1.0, 0.0).astype(BF16)
    rt_ref[...] = jnp.dot(order, rg[...].reshape(ring * padded, cols), preferred_element_type=F32).astype(BF16)

    for copy in spread:
        copy.wait_send()
    for copy in flights.values():
        copy.wait_send()


def combine_kernel(unroll, q_ref, rt_ref, in_ref, out_ref, term_ref, p_ref, b_ref):
    tasks = in_ref.shape[0]
    lanes = q_ref.shape[3]
    per = lanes // 8
    b_ref[...] = jnp.zeros_like(b_ref)
    group = lax.broadcasted_iota(jnp.int32, q_ref.shape[2:], 1) // per

    def step(n, carry):
        moved = []
        for u in range(unroll):
            t = n * unroll + u
            s, w, r = in_ref[t], term_ref[t], out_ref[t]
            block = q_ref[w, s // 8]
            shift = ((w - s + 64) % 8) * per
            block = pltpu.roll(block, shift, axis=1)
            moved.append((r, w // 8, jnp.where(group == w % 8, block, 0.0)))
        for r, tile, block in moved:
            b_ref[r, tile] = b_ref[r, tile] + block
        return carry

    lax.fori_loop(0, tasks // unroll, step, 0)

    sectors, tiles, rows, _ = b_ref.shape
    chunk = 8
    for c in range(sectors // chunk):
        b = jnp.concatenate([b_ref[c * chunk : (c + 1) * chunk, k] for k in range(tiles)], axis=2)
        b = b.reshape(chunk * rows, tiles * lanes)
        top = b.astype(BF16)
        rest = (b - top.astype(F32)).astype(BF16)
        p = jnp.dot(top, rt_ref[...], preferred_element_type=F32) + jnp.dot(
            rest, rt_ref[...], preferred_element_type=F32
        )
        p_ref[c * (chunk // 2) : (c + 1) * (chunk // 2)] = p.reshape(chunk // 2, 2, rows, p.shape[1])


def scatter_kernel(p_ref, o_ref, pair, acc, xa, yb, ca, cb, ya, xb, send, recv):
    g = lax.axis_index("sec")
    core = lax.rem(g, 2)
    x = lax.rem(g // 2, 4)
    y = g // 8
    sibling = g + 1 - 2 * core
    half = o_ref.shape[1] // 2

    def x_peer(d):
        return (y * 4 + lax.rem(x + d, 4)) * 2 + core

    def y_peer(d):
        return (lax.rem(y + d, 4) * 4 + x) * 2 + core

    barrier = pltpu.get_barrier_semaphore()
    peers = [sibling] + [x_peer(d) for d in (1, 2, 3)] + [y_peer(d) for d in (1, 2, 3)]
    for to in peers:
        pl.semaphore_signal(barrier, inc=1, device_id={"sec": to}, device_id_type=MESH)
    pl.semaphore_wait(barrier, len(peers))

    def copy(src, dst, index, to):
        made = pltpu.make_async_remote_copy(
            src_ref=src,
            dst_ref=dst,
            send_sem=send.at[index],
            recv_sem=recv.at[index],
            device_id={"sec": to},
            device_id_type=MESH,
        )
        made.start()
        return made

    tops = slice(0, half), slice(half, 2 * half)
    first = [
        copy(p_ref.at[:, 1 - core, pl.ds(k * half, half)], pair.at[k], k, sibling) for k in range(2)
    ]
    second, third = [], []
    for k in range(2):
        first[k].wait_recv()
        acc[k] = (p_ref[:, core, tops[k]] + pair[k]).reshape(acc.shape[1:])
        for d in (1, 2, 3):
            index = 2 + k * 3 + d - 1
            if k == 0:
                second.append(copy(acc.at[0, :, lax.rem(x + d, 4)], xa.at[d - 1], index, x_peer(d)))
            else:
                second.append(copy(acc.at[1, lax.rem(y + d, 4)], yb.at[d - 1], index, y_peer(d)))
    for k in range(2):
        for d in (1, 2, 3):
            second[k * 3 + d - 1].wait_recv()
        if k == 0:
            ca[...] = acc[0, :, x] + xa[0] + xa[1] + xa[2]
        else:
            cb[...] = acc[1, y] + yb[0] + yb[1] + yb[2]
        for d in (1, 2, 3):
            index = 8 + k * 3 + d - 1
            if k == 0:
                third.append(copy(ca.at[lax.rem(y + d, 4)], ya.at[d - 1], index, y_peer(d)))
            else:
                third.append(copy(cb.at[lax.rem(x + d, 4)], xb.at[d - 1], index, x_peer(d)))
    for k in range(2):
        for d in (1, 2, 3):
            third[k * 3 + d - 1].wait_recv()
        if k == 0:
            o_ref[0, :half] = ca[y] + ya[0] + ya[1] + ya[2]
        else:
            o_ref[0, half:] = cb[x] + xb[0] + xb[1] + xb[2]
    for made in first + second + third:
        made.wait_send()


def body(wavefunction, left_env, right_env, task_in, task_out, task_term):
    groups = lax.axis_size("sec")
    ring = lax.axis_size("env")
    _, rows, cols = wavefunction.shape
    terms = left_env.shape[0]
    per = cols // groups
    padded = -(-terms // 16) * 16
    tiles = -(-terms // 8)
    limit = 48 * 2**20
    sems = pltpu.SemaphoreType.DMA

    q, rt = pl.pallas_call(
        functools.partial(gather_kernel, groups, ring),
        out_shape=(
            jax.ShapeDtypeStruct((terms, groups // 8, rows, 128), F32),
            jax.ShapeDtypeStruct((tiles * 128, cols), BF16),
        ),
        in_specs=[vmem()] * 3,
        out_specs=(vmem(), vmem()),
        scratch_shapes=[
            pltpu.VMEM((cols, 128), F32),
            pltpu.VMEM((groups, per, 128), BF16),
            pltpu.VMEM((groups, per, 128), BF16),
            pltpu.VMEM((ring, 2 * rows, cols), BF16),
            pltpu.VMEM((ring, padded, cols), BF16),
            pltpu.VMEM((padded, cols), F32),
            sems((groups,)),
            sems((groups,)),
            sems((2 * ring,)),
            sems((2 * ring,)),
        ],
        compiler_params=pltpu.CompilerParams(collective_id=0, has_side_effects=True, vmem_limit_bytes=limit),
        name="gather_psi",
    )(wavefunction, left_env, right_env)

    smem = pl.BlockSpec(memory_space=pltpu.SMEM)
    partial = pl.pallas_call(
        functools.partial(combine_kernel, 8),
        out_shape=jax.ShapeDtypeStruct((groups // 2, 2, rows, cols), F32),
        in_specs=[vmem(), vmem(), smem, smem, smem],
        out_specs=vmem(),
        scratch_shapes=[pltpu.VMEM((groups, tiles, rows, 128), F32)],
        compiler_params=pltpu.CompilerParams(vmem_limit_bytes=limit),
        name="combine_tasks",
    )(q, rt, task_in, task_out[:, 0], task_term)

    half = rows // 2
    return pl.pallas_call(
        scatter_kernel,
        out_shape=jax.ShapeDtypeStruct((1, rows, cols), F32),
        in_specs=[vmem()],
        out_specs=vmem(),
        scratch_shapes=[
            pltpu.VMEM((2, 16, half, cols), F32),
            pltpu.VMEM((2, 4, 4, half, cols), F32),
            pltpu.VMEM((3, 4, half, cols), F32),
            pltpu.VMEM((3, 4, half, cols), F32),
            pltpu.VMEM((4, half, cols), F32),
            pltpu.VMEM((4, half, cols), F32),
            pltpu.VMEM((3, half, cols), F32),
            pltpu.VMEM((3, half, cols), F32),
            sems((14,)),
            sems((14,)),
        ],
        compiler_params=pltpu.CompilerParams(collective_id=1, has_side_effects=True, vmem_limit_bytes=limit),
        name="scatter_sums",
    )(partial)


def solution(mesh):
    placed = (P("sec", "env", None), P(None, "env", None), P(None, "env", None), P(), P(), P())
    return jax.shard_map(
        body, mesh=mesh, in_specs=placed, out_specs=P("sec", "env", None), check_vma=False
    )
```

time: 259 us -> 88.7 us (0.34)
  blocking collectives: 201 us -> 0 us
  Pallas kernels: 0 us -> 84.5 us
  waiting for transfers between devices: 23.6 us -> 0 us
  starting transfers between devices: 10.7 us -> 0 us
  local copies, waits for them, and re-layouts: 12.2 us -> 3.98 us
  other arithmetic: 6.69 us -> 0 us
  matrix products: 3.35 us -> 0 us
    all_to_all x3 -> x0, blocking collectives: 201 us -> none  [the longest x1 102 us: sent_together(): lax.all_to_all(both, axis, split_axis=split_dim, concat_axis=concat_dim,...]
    pallas_call x0 -> x3, Pallas kernels: none -> 84.5 us  [the longest x1 48.4 us: body(): pl.pallas_call(functools.partial(gather_kernel, groups, ring), out_shape=...]
    all_to_all x1 -> x0, waiting for transfers between devices: 23.6 us -> none  [from_everyone(): return lax.all_to_all(copies, axis, split_axis=0, concat_axis=0, tiled=True)]
    all_to_all x1 -> x0, starting transfers between devices: 10.7 us -> none  [from_everyone(): return lax.all_to_all(copies, axis, split_axis=0, concat_axis=0, tiled=True)]
    gather x4 -> x0, local copies, waits for them, and re-layouts: 8.43 us -> none  [the longest x1 2.64 us: outgoing(): right_send = jnp.take(right_env, term_ids, axis=0)]
    unnamed x8 -> x13, local copies, waits for them, and re-layouts: 0.02 us -> 3.98 us
    convert_element_type x2 -> x0, other arithmetic: 3.76 us -> none  [the longest x1 2.6 us: body(): low_rows = (all_rows - high_rows.astype(jnp.float32)).astype(jnp.bfloat16)]
    dot_general x5 -> x0, matrix products: 3.35 us -> none  [the longest x1 1.58 us: even_slot(): jnp.einsum('gk,krc->grc', target_hits, received, precision=lax.Precision....]
  transfers between devices with their start and end apart: 1 -> 0, of which waited for: 1 -> 0; matrix products, arithmetic and copies ran while one was open for 2% -> 0% of each run, Pallas kernels for 0% -> 0%
where the time goes in v1:
time: 88.7 us; the launch traced here: 88.5 us
  Pallas kernels  84.5 us (95%)
  local copies, waits for them, and re-layouts  3.98 us (4%)
    pallas_call x1, Pallas kernels, body(): pl.pallas_call(functools.partial(gather_kernel, groups, ring), out_shape=...  48.4 us
    pallas_call x1, Pallas kernels, body(): pl.pallas_call(scatter_kernel, out_shape=jax.ShapeDtypeStruct((1, rows, c...  23.8 us
    pallas_call x1, Pallas kernels, body(): pl.pallas_call(functools.partial(combine_kernel, 8), out_shape=jax.ShapeD...  12.3 us
    unnamed x13, local copies, waits for them, and re-layouts  3.98 us

profile of v1, /device:TPU:1, one launch (start us, length us, event | category | flops | bytes accessed | tf_op | source)
XLA Modules:
  0.0 88.5 jit_solution(6234473456207889198)
XLA Ops:
  0.0 0.0 copy-start
  0.0 1.2 %copy-done = bf16[34,32,512]{2,1,0:T(8,128)(2,1)S(1)} copy-done((bf16[34,32,512]{2,1,0:T(8,128)(2,1)S(1)}, bf16[34,32,512]{2,1,0:T(8,128)(2,1)}, u32[]{:S(2)}) %copy-start) | copy-done | bytes 1114136
  1.2 0.0 copy-start.1
  1.3 1.2 %copy-done.1 = bf16[34,32,512]{2,1,0:T(8,128)(2,1)S(1)} copy-done((bf16[34,32,512]{2,1,0:T(8,128)(2,1)S(1)}, bf16[34,32,512]{2,1,0:T(8,128)(2,1)}, u32[]{:S(2)}) %copy-start.1) | copy-done | bytes 1114136
  2.5 0.0 copy-start.2
  2.5 0.8 copy-done.2
  3.3 0.0 copy-start.3
  3.3 0.0 copy-start.4
  3.3 0.0 copy-start.5
  3.3 48.4 %gather_psi.1 = (f32[34,4,32,128]{3,2,1,0:T(8,128)S(1)}, bf16[640,512]{1,0:T(8,128)(2,1)S(1)}) custom-call(f32[1,32,512]{2,1,0:T(8,128)S(1)} %copy-done.2, bf16[34,32,512]{2,1,0:T(8,128)(2,1)S(1)} %copy-done, bf16[34,32,512]{2,1,0:T(8,128)(2,1)S(1)} %copy-done.1), custom_call_target="tpu_custom_call" | custom-call | tf_op jit(solution)/shard_map/gather_psi/pallas_call | solution.py:241
  51.7 0.0 copy-done.3
  51.7 0.0 copy-done.4
  51.7 0.0 copy-done.5
  51.8 12.3 %combine_tasks.1.p_ref = f32[16,2,32,512]{3,2,1,0:T(8,128)S(1)} custom-call(f32[34,4,32,128]{3,2,1,0:T(8,128)S(1)} %get-tuple-element.7.q_ref, bf16[640,512]{1,0:T(8,128)(2,1)S(1)} %get-tuple-element.8.rt_ref, s32[512]{0:T(512)S(1)} %copy-done.3, s32[512]{0:T(512)S(1)} %bitcast.1, s32[512]{0:T(512)S(1)} %copy-done.5), custom_call_target="tpu_custom_call" | custom-call | tf_op jit(solution)/shard_map/combine_tasks/pallas_call | solution.py:266
  64.0 23.8 %scatter_sums.1 = f32[1,32,512]{2,1,0:T(8,128)S(1)} custom-call(f32[16,2,32,512]{3,2,1,0:T(8,128)S(1)} %combine_tasks.1.p_ref), custom_call_target="tpu_custom_call" | custom-call | tf_op jit(solution)/shard_map/scatter_sums/pallas_call | solution.py:277
  87.9 0.6 copy.8
Async XLA Ops:
  0.0 1.2 %copy-start = (bf16[34,32,512]{2,1,0:T(8,128)(2,1)S(1)}, bf16[34,32,512]{2,1,0:T(8,128)(2,1)}, u32[]{:S(2)}) copy-start(bf16[34,32,512]{2,1,0:T(8,128)(2,1)} %left_ref.1) | copy-start | bytes 3342340
  1.2 1.2 %copy-start.1 = (bf16[34,32,512]{2,1,0:T(8,128)(2,1)S(1)}, bf16[34,32,512]{2,1,0:T(8,128)(2,1)}, u32[]{:S(2)}) copy-start(bf16[34,32,512]{2,1,0:T(8,128)(2,1)} %right_ref.1) | copy-start | bytes 3342340
  2.5 0.8 copy-start.2
  3.3 48.4 %copy-start.3 = (s32[512]{0:T(512)S(1)}, s32[512]{0:T(512)}, u32[]{:S(2)}) copy-start(s32[512]{0:T(512)} %in_ref.1) | copy-start | bytes 6148
  3.3 48.4 %copy-start.4 = (s32[512,1]{0,1:T(1,128)S(1)}, s32[512,1]{0,1:T(1,128)}, u32[]{:S(2)}) copy-start(s32[512,1]{0,1:T(1,128)} %param.10) | copy-start | bytes 6148
  3.3 48.4 %copy-start.5 = (s32[512]{0:T(512)S(1)}, s32[512]{0:T(512)}, u32[]{:S(2)}) copy-start(s32[512]{0:T(512)} %term_ref.1) | copy-start | bytes 6148

commit v2 on v1

v2 whole, which is shorter than its diff:
```python
import functools

import jax
import jax.numpy as jnp
from jax import lax
from jax.experimental import pallas as pl
from jax.experimental.pallas import tpu as pltpu
from jax.sharding import PartitionSpec as P

MESH = pl.DeviceIdType.MESH
F32 = jnp.float32
BF16 = jnp.bfloat16


def vmem():
    return pl.BlockSpec(memory_space=pltpu.VMEM)


def gather_kernel(groups, ring, psi_hbm, left_hbm, right_hbm, in_hbm, out_hbm, term_hbm, q_ref, rt_ref, pk_ref,
                  psi_ref, left_ref, right_ref, ids, t_scr, send_buf, got, hl, rg, rrow,
                  a_send, a_recv, z_send, z_recv, local):
    g = lax.axis_index("sec")
    e = lax.axis_index("env")
    terms = left_ref.shape[0]
    rows = psi_ref.shape[1]
    cols = psi_ref.shape[2]
    per = cols // groups
    right = lax.rem(e + 1, ring)
    left = lax.rem(e + ring - 1, ring)

    loads = [
        pltpu.make_async_copy(src, dst, local.at[n])
        for n, (src, dst) in enumerate(
            (
                (psi_hbm, psi_ref),
                (right_hbm, right_ref),
                (in_hbm, ids.at[0]),
                (out_hbm, ids.at[1]),
                (term_hbm, ids.at[2]),
                (left_hbm, left_ref),
            )
        )
    ]
    for load in loads:
        load.start()

    barrier = pltpu.get_barrier_semaphore()
    for d in range(1, groups):
        pl.semaphore_signal(barrier, inc=1, device_id={"sec": lax.rem(g + d, groups)}, device_id_type=MESH)
    for to in (left, right):
        pl.semaphore_signal(barrier, inc=1, device_id={"env": to}, device_id_type=MESH)

    loads[0].wait()
    psi = psi_ref[0]
    high = psi.astype(BF16)
    low = (psi - high.astype(F32)).astype(BF16)
    stacked = jnp.concatenate(
        [high.astype(F32), low.astype(F32), jnp.zeros((128 - 2 * rows, cols), F32)], axis=0
    )
    t_scr[...] = stacked.T
    for p in range(groups):
        send_buf[p] = t_scr[pl.ds(p, per, stride=groups), :].astype(BF16)

    pl.semaphore_wait(barrier, groups + 1)

    spread = []
    for d in range(1, groups):
        to = lax.rem(g + d, groups)
        copy = pltpu.make_async_remote_copy(
            src_ref=send_buf.at[to],
            dst_ref=got.at[g],
            send_sem=a_send.at[d],
            recv_sem=a_recv.at[d],
            device_id={"sec": to},
            device_id_type=MESH,
        )
        copy.start()
        spread.append(copy)
    got[g] = send_buf[g]

    loads[1].wait()
    rrow[...] = jnp.zeros_like(rrow)
    pick = lax.broadcasted_iota(jnp.int32, (rows, cols), 0) == g
    for w in range(terms):
        row = jnp.sum(jnp.where(pick, right_ref[w].astype(F32), 0.0), axis=0, keepdims=True)
        rrow[pl.ds(w, 1), :] = row
    rg[e] = rrow[...].astype(BF16)

    steps = ring // 2
    ways = ((right, -1, steps), (left, 1, steps - 1))
    flights = {}

    def forward(buffer, b, n, h):
        for way, (to, sign, hops) in enumerate(ways):
            if (way, b, n, h - 1) in flights:
                flights[way, b, n, h - 1].wait_recv()
            if h < hops:
                slot = lax.rem(e + sign * h + ring, ring)
                part = buffer.at[slot, pl.ds(n * 16, 16)]
                index = ((b * 4 + n) * 2 + way) * steps + h
                copy = pltpu.make_async_remote_copy(
                    src_ref=part,
                    dst_ref=part,
                    send_sem=z_send.at[index],
                    recv_sem=z_recv.at[index],
                    device_id={"env": to},
                    device_id_type=MESH,
                )
                copy.start()
                flights[way, b, n, h] = copy

    psi_parts = hl.shape[1] // 16
    right_parts = rg.shape[1] // 16
    for n in range(right_parts):
        forward(rg, 1, n, 0)

    for load in loads[2:5]:
        load.wait()
    s, r, w = ids[0], ids[1], ids[2]
    pk_ref[...] = (
        w * 4 + (s >> 3)
        + ((r * (rt_ref.shape[0] // 128) + (w >> 3)) << 8)
        + (((w - s) & 7) << 16)
        + ((w & 7) << 20)
    )

    for copy in spread:
        copy.wait_recv()
    back = got[...].astype(F32).reshape(groups * per, 128).T
    hl[e] = back[: 2 * rows].astype(BF16)

    for h in range(steps + 1):
        for n in range(psi_parts):
            if h < steps:
                forward(hl, 0, n, h)
        if h < steps:
            for n in range(right_parts):
                forward(rg, 1, n, h + 1)

    padded = rg.shape[1]
    out_row = lax.broadcasted_iota(jnp.int32, (rt_ref.shape[0], ring * padded), 0)
    in_row = lax.broadcasted_iota(jnp.int32, (rt_ref.shape[0], ring * padded), 1)
    same = (out_row // ring == in_row % padded) & (out_row % ring == in_row // padded) & (out_row < terms * ring)
    order = jnp.where(same, 1.0, 0.0).astype(BF16)
    rt_ref[...] = jnp.dot(order, rg[...].reshape(ring * padded, cols), preferred_element_type=F32).astype(BF16)

    loads[5].wait()
    for n in range(psi_parts):
        forward(hl, 0, n, steps)
    block = cols // 2
    lanes = q_ref.shape[3]
    lhs = left_ref[...].reshape(terms * rows, cols)
    for half in range(2):
        x_high = hl[:, :rows, half * block : (half + 1) * block].reshape(ring * rows, block)
        x_low = hl[:, rows:, half * block : (half + 1) * block].reshape(ring * rows, block)
        q = jnp.dot(lhs, x_high, preferred_element_type=F32) + jnp.dot(lhs, x_low, preferred_element_type=F32)
        for part in range(block // lanes):
            q_ref[:, half * (block // lanes) + part] = q[:, part * lanes : (part + 1) * lanes].reshape(
                terms, rows, lanes
            )

    for copy in spread:
        copy.wait_send()
    for copy in flights.values():
        copy.wait_send()


def combine_kernel(unroll, q_ref, pk_ref, b0_ref, b1_ref):
    tasks = pk_ref.shape[0] * pk_ref.shape[1]
    lanes = q_ref.shape[-1]
    per = lanes // 8
    b0_ref[...] = jnp.zeros_like(b0_ref)
    b1_ref[...] = jnp.zeros_like(b1_ref)
    shape = q_ref.shape[1:]
    group = lax.broadcasted_iota(jnp.int32, shape, 2) // per

    def step(n, carry):
        moved = []
        for u in range(unroll):
            t = n * unroll + u
            word = pk_ref[t // 128, t % 128]
            block = q_ref[word & 255].reshape(shape[0] * shape[1], lanes)
            block = pltpu.roll(block, ((word >> 16) & 15) * per, axis=1).reshape(shape)
            moved.append(((word >> 8) & 255, jnp.where(group == (word >> 20), block, 0.0)))
        for u, (place, block) in enumerate(moved):
            b_ref = (b0_ref, b1_ref)[u % 2]
            b_ref[place] = b_ref[place] + block
        return carry

    lax.fori_loop(0, tasks // unroll, step, 0)


def scatter_kernel(b0_ref, b1_ref, rt_ref, o_ref, mine, pair, acc, xa, yb, ca, cb, ya, xb, send, recv):
    g = lax.axis_index("sec")
    core = lax.rem(g, 2)
    x = lax.rem(g // 2, 4)
    y = g // 8
    sibling = g + 1 - 2 * core
    half = o_ref.shape[1] // 2
    tiles = b0_ref.shape[2]

    def x_peer(d):
        return (y * 4 + lax.rem(x + d, 4)) * 2 + core

    def y_peer(d):
        return (lax.rem(y + d, 4) * 4 + x) * 2 + core

    barrier = pltpu.get_barrier_semaphore()
    peers = [sibling] + [x_peer(d) for d in (1, 2, 3)] + [y_peer(d) for d in (1, 2, 3)]
    for to in peers:
        pl.semaphore_signal(barrier, inc=1, device_id={"sec": to}, device_id_type=MESH)

    def product(parity, k):
        at = pl.ds(k * half, half)
        b = jnp.concatenate(
            [b0_ref[:, parity, n, at] + b1_ref[:, parity, n, at] for n in range(tiles)], axis=2
        )
        b = b.reshape(b.shape[0] * half, b.shape[2])
        top = b.astype(BF16)
        rest = (b - top.astype(F32)).astype(BF16)
        return jnp.dot(top, rt_ref[...], preferred_element_type=F32) + jnp.dot(
            rest, rt_ref[...], preferred_element_type=F32
        )

    def copy(src, dst, index, to):
        made = pltpu.make_async_remote_copy(
            src_ref=src,
            dst_ref=dst,
            send_sem=send.at[index],
            recv_sem=recv.at[index],
            device_id={"sec": to},
            device_id_type=MESH,
        )
        made.start()
        return made

    first, second, third = [], [], []
    for k in range(2):
        mine[k] = product(1 - core, k).reshape(mine.shape[1:])
        if k == 0:
            pl.semaphore_wait(barrier, len(peers))
        first.append(copy(mine.at[k], pair.at[k], k, sibling))
    for k in range(2):
        own = product(core, k).reshape(acc.shape[1:])
        first[k].wait_recv()
        acc[k] = own + pair[k].reshape(acc.shape[1:])
        for d in (2, 1, 3):
            index = 2 + k * 3 + d - 1
            if k == 0:
                second.append(copy(acc.at[0, :, lax.rem(x + d, 4)], xa.at[d - 1], index, x_peer(d)))
            else:
                second.append(copy(acc.at[1, lax.rem(y + d, 4)], yb.at[d - 1], index, y_peer(d)))
    for k in range(2):
        for d in (1, 2, 3):
            second[k * 3 + d - 1].wait_recv()
        if k == 0:
            ca[...] = acc[0, :, x] + xa[0] + xa[1] + xa[2]
        else:
            cb[...] = acc[1, y] + yb[0] + yb[1] + yb[2]
        for d in (2, 1, 3):
            index = 8 + k * 3 + d - 1
            if k == 0:
                third.append(copy(ca.at[lax.rem(y + d, 4)], ya.at[d - 1], index, y_peer(d)))
            else:
                third.append(copy(cb.at[lax.rem(x + d, 4)], xb.at[d - 1], index, x_peer(d)))
    for k in range(2):
        for d in (1, 2, 3):
            third[k * 3 + d - 1].wait_recv()
        if k == 0:
            o_ref[0, :half] = ca[y] + ya[0] + ya[1] + ya[2]
        else:
            o_ref[0, half:] = cb[x] + xb[0] + xb[1] + xb[2]
    for made in first + second + third:
        made.wait_send()


def body(wavefunction, left_env, right_env, task_in, task_out, task_term):
    groups = lax.axis_size("sec")
    ring = lax.axis_size("env")
    _, rows, cols = wavefunction.shape
    terms = left_env.shape[0]
    per = cols // groups
    padded = -(-terms // 16) * 16
    tiles = -(-terms // 8)
    limit = 40 * 2**20
    sems = pltpu.SemaphoreType.DMA
    ids = (task_in.shape[0] // 128, 128)
    hbm = pl.BlockSpec(memory_space=pltpu.HBM)

    q, rt, packed = pl.pallas_call(
        functools.partial(gather_kernel, groups, ring),
        out_shape=(
            jax.ShapeDtypeStruct((terms, groups // 8, rows, 128), F32),
            jax.ShapeDtypeStruct((tiles * 128, cols), BF16),
            jax.ShapeDtypeStruct(ids, jnp.int32),
        ),
        in_specs=[hbm] * 6,
        out_specs=(vmem(), vmem(), vmem()),
        scratch_shapes=[
            pltpu.VMEM(wavefunction.shape, F32),
            pltpu.VMEM(left_env.shape, BF16),
            pltpu.VMEM(right_env.shape, BF16),
            pltpu.VMEM((3, *ids), jnp.int32),
            pltpu.VMEM((cols, 128), F32),
            pltpu.VMEM((groups, per, 128), BF16),
            pltpu.VMEM((groups, per, 128), BF16),
            pltpu.VMEM((ring, 2 * rows, cols), BF16),
            pltpu.VMEM((ring, padded, cols), BF16),
            pltpu.VMEM((padded, cols), F32),
            sems((groups,)),
            sems((groups,)),
            sems((8 * ring,)),
            sems((8 * ring,)),
            sems((6,)),
        ],
        compiler_params=pltpu.CompilerParams(collective_id=0, has_side_effects=True, vmem_limit_bytes=limit),
        name="gather_psi",
    )(*(
        pltpu.with_memory_space_constraint(a, pltpu.HBM)
        for a in (wavefunction, left_env, right_env, task_in.reshape(ids), task_out.reshape(ids), task_term.reshape(ids))
    ))

    sums = jax.ShapeDtypeStruct((groups * tiles, rows // 8, 8, 128), F32)
    even, odd = pl.pallas_call(
        functools.partial(combine_kernel, 16),
        out_shape=(sums, sums),
        in_specs=[vmem(), pl.BlockSpec(memory_space=pltpu.SMEM)],
        out_specs=(vmem(), vmem()),
        compiler_params=pltpu.CompilerParams(vmem_limit_bytes=limit),
        name="combine_tasks",
    )(q.reshape(terms * (groups // 8), rows // 8, 8, 128), packed)

    half = rows // 2
    split = (groups // 2, 2, tiles, rows, 128)
    return pl.pallas_call(
        scatter_kernel,
        out_shape=jax.ShapeDtypeStruct((1, rows, cols), F32),
        in_specs=[vmem()] * 3,
        out_specs=vmem(),
        scratch_shapes=[
            pltpu.VMEM((2, 16, half, cols), F32),
            pltpu.VMEM((2, 16, half, cols), F32),
            pltpu.VMEM((2, 4, 4, half, cols), F32),
            pltpu.VMEM((3, 4, half, cols), F32),
            pltpu.VMEM((3, 4, half, cols), F32),
            pltpu.VMEM((4, half, cols), F32),
            pltpu.VMEM((4, half, cols), F32),
            pltpu.VMEM((3, half, cols), F32),
            pltpu.VMEM((3, half, cols), F32),
            sems((14,)),
            sems((14,)),
        ],
        compiler_params=pltpu.CompilerParams(collective_id=1, has_side_effects=True, vmem_limit_bytes=limit),
        name="scatter_sums",
    )(even.reshape(split), odd.reshape(split), rt)


def solution(mesh):
    placed = (P("sec", "env", None), P(None, "env", None), P(None, "env", None), P(), P(), P())
    return jax.shard_map(
        body, mesh=mesh, in_specs=placed, out_specs=P("sec", "env", None), check_vma=False
    )
```

time: 88.7 us -> 76.2 us (0.86)
  Pallas kernels: 84.5 us -> 75.4 us
  local copies, waits for them, and re-layouts: 3.98 us -> 0.63 us
    pallas_call x1, Pallas kernels: 12.3 us -> 7.4 us  [body(): pl.pallas_call(functools.partial(combine_kernel, 16), out_shape=(sums, su...]
    unnamed x13 -> x1, local copies, waits for them, and re-layouts: 3.98 us -> 0.63 us
    pallas_call x1, Pallas kernels: 48.4 us -> 45.5 us  [body(): pl.pallas_call(functools.partial(gather_kernel, groups, ring), out_shape=...]
    pallas_call x1, Pallas kernels: 23.8 us -> 22.5 us  [body(): pl.pallas_call(scatter_kernel, out_shape=jax.ShapeDtypeStruct((1, rows, c...]
where the time goes in v2:
time: 76.2 us; the launch traced here: 76.1 us
  Pallas kernels  75.4 us (99%)
    pallas_call x1, Pallas kernels, body(): pl.pallas_call(functools.partial(gather_kernel, groups, ring), out_shape=...  45.5 us
    pallas_call x1, Pallas kernels, body(): pl.pallas_call(scatter_kernel, out_shape=jax.ShapeDtypeStruct((1, rows, c...  22.5 us
    pallas_call x1, Pallas kernels, body(): pl.pallas_call(functools.partial(combine_kernel, 16), out_shape=(sums, su...  7.4 us

profile of v2, /device:TPU:1, one launch (start us, length us, event | category | flops | bytes accessed | tf_op | source)
XLA Modules:
  0.0 76.1 jit_solution(12336238995585887912)
XLA Ops:
  0.0 45.5 %gather_psi.1 = (f32[34,4,32,128]{3,2,1,0:T(8,128)S(1)}, bf16[640,512]{1,0:T(8,128)(2,1)S(1)}, s32[4,128]{1,0:T(4,128)S(1)}) custom-call(f32[1,32,512]{2,1,0:T(8,128)} %psi_hbm.1, bf16[34,32,512]{2,1,0:T(8,128)(2,1)} %left_hbm.1, bf16[34,32,512]{2,1,0:T(8,128)(2,1)} %right_hbm.1, s32[4,128]{1,0:T(4,128)} %bitcast.9, s32[4,128]{1,0:T(4,128)} %bitcast.10, ...), custom_call_target="tpu_custom_call" | custom-call | tf_op jit(solution)/shard_map/gather_psi/pallas_call | solution.py:290
  45.5 7.4 %combine_tasks.1 = (f32[160,4,8,128]{3,2,1,0:T(8,128)S(1)}, f32[160,4,8,128]{3,2,1,0:T(8,128)S(1)}) custom-call(f32[136,4,8,128]{3,2,1,0:T(8,128)S(1)} %bitcast.8, s32[4,128]{1,0:T(4,128)S(1)} %get-tuple-element.11.pk_ref), custom_call_target="tpu_custom_call" | custom-call | tf_op jit(solution)/shard_map/combine_tasks/pallas_call | solution.py:324
  52.9 22.5 %scatter_sums.1 = f32[1,32,512]{2,1,0:T(8,128)S(1)} custom-call(f32[16,2,5,32,128]{4,3,2,1,0:T(8,128)S(1)} %bitcast.6, f32[16,2,5,32,128]{4,3,2,1,0:T(8,128)S(1)} %bitcast.7, bf16[640,512]{1,0:T(8,128)(2,1)S(1)} %get-tuple-element.14.rt_ref), custom_call_target="tpu_custom_call" | custom-call | tf_op jit(solution)/shard_map/scatter_sums/pallas_call | solution.py:335
  75.4 0.6 copy.8

commit v3 on v2

--- a/solution.py
+++ b/solution.py
@@ -17,7 +17,7 @@
 
 
 def gather_kernel(groups, ring, psi_hbm, left_hbm, right_hbm, in_hbm, out_hbm, term_hbm, q_ref, rt_ref, pk_ref,
-                  psi_ref, left_ref, right_ref, ids, t_scr, send_buf, got, hl, rg, rrow,
+                  psi_ref, left_ref, right_ref, ids, t_scr, send_buf, got, hl, rg, rg_last, rrow,
                   a_send, a_recv, z_send, z_recv, local):
     g = lax.axis_index("sec")
     e = lax.axis_index("env")
@@ -27,6 +27,9 @@
     per = cols // groups
     right = lax.rem(e + 1, ring)
     left = lax.rem(e + ring - 1, ring)
+    jump = ring // 4
+    far_right = lax.rem(e + jump, ring)
+    far_left = lax.rem(e + ring - jump, ring)
 
     loads = [
         pltpu.make_async_copy(src, dst, local.at[n])
@@ -47,7 +50,7 @@
     barrier = pltpu.get_barrier_semaphore()
     for d in range(1, groups):
         pl.semaphore_signal(barrier, inc=1, device_id={"sec": lax.rem(g + d, groups)}, device_id_type=MESH)
-    for to in (left, right):
+    for to in (left, right, far_left, far_right):
         pl.semaphore_signal(barrier, inc=1, device_id={"env": to}, device_id_type=MESH)
 
     loads[0].wait()
@@ -61,7 +64,7 @@
     for p in range(groups):
         send_buf[p] = t_scr[pl.ds(p, per, stride=groups), :].astype(BF16)
 
-    pl.semaphore_wait(barrier, groups + 1)
+    pl.semaphore_wait(barrier, groups + 3)
 
     spread = []
     for d in range(1, groups):
@@ -78,41 +81,56 @@
         spread.append(copy)
     got[g] = send_buf[g]
 
+    main = rg.shape[1]
     loads[1].wait()
     rrow[...] = jnp.zeros_like(rrow)
     pick = lax.broadcasted_iota(jnp.int32, (rows, cols), 0) == g
     for w in range(terms):
         row = jnp.sum(jnp.where(pick, right_ref[w].astype(F32), 0.0), axis=0, keepdims=True)
         rrow[pl.ds(w, 1), :] = row
-    rg[e] = rrow[...].astype(BF16)
+    rg[e] = rrow[:main].astype(BF16)
 
     steps = ring // 2
-    ways = ((right, -1, steps), (left, 1, steps - 1))
     flights = {}
-
-    def forward(buffer, b, n, h):
-        for way, (to, sign, hops) in enumerate(ways):
-            if (way, b, n, h - 1) in flights:
-                flights[way, b, n, h - 1].wait_recv()
-            if h < hops:
-                slot = lax.rem(e + sign * h + ring, ring)
-                part = buffer.at[slot, pl.ds(n * 16, 16)]
-                index = ((b * 4 + n) * 2 + way) * steps + h
-                copy = pltpu.make_async_remote_copy(
-                    src_ref=part,
-                    dst_ref=part,
-                    send_sem=z_send.at[index],
-                    recv_sem=z_recv.at[index],
-                    device_id={"env": to},
-                    device_id_type=MESH,
-                )
-                copy.start()
-                flights[way, b, n, h] = copy
-
-    psi_parts = hl.shape[1] // 16
-    right_parts = rg.shape[1] // 16
-    for n in range(right_parts):
-        forward(rg, 1, n, 0)
+    used = []
+
+    def forward(chain, h):
+        key, buffer, hops, place = chain
+        if (key, h - 1) in flights:
+            flights[key, h - 1].wait_recv()
+        if h < hops:
+            off, to = place(h)
+            part = buffer.at[lax.rem(e + off + ring, ring)]
+            index = len(used)
+            used.append(index)
+            copy = pltpu.make_async_remote_copy(
+                src_ref=part,
+                dst_ref=part,
+                send_sem=z_send.at[index],
+                recv_sem=z_recv.at[index],
+                device_id={"env": to},
+                device_id_type=MESH,
+            )
+            copy.start()
+            flights[key, h] = copy
+
+    def chains(key, buffer):
+        return (
+            (key + "br", buffer, steps - jump + 1, lambda h: (1 - jump - h, right) if h else (0, far_right)),
+            (key + "bl", buffer, steps - jump, lambda h: (jump - 1 + h, left) if h else (0, far_left)),
+            (key + "ar", buffer, jump - 1, lambda h: (-h, right)),
+            (key + "al", buffer, jump - 1, lambda h: (h, left)),
+        )
+
+    psi_chains = chains("p", hl) + chains("t", rg_last)
+    right_chains = chains("m", rg)
+    last_step = steps - jump + 1
+
+    def move(group, h):
+        for chain in group:
+            forward(chain, h)
+
+    move(right_chains, 0)
 
     for load in loads[2:5]:
         load.wait()
@@ -127,37 +145,63 @@
     for copy in spread:
         copy.wait_recv()
     back = got[...].astype(F32).reshape(groups * per, 128).T
-    hl[e] = back[: 2 * rows].astype(BF16)
-
-    for h in range(steps + 1):
-        for n in range(psi_parts):
-            if h < steps:
-                forward(hl, 0, n, h)
-        if h < steps:
-            for n in range(right_parts):
-                forward(rg, 1, n, h + 1)
-
-    padded = rg.shape[1]
-    out_row = lax.broadcasted_iota(jnp.int32, (rt_ref.shape[0], ring * padded), 0)
-    in_row = lax.broadcasted_iota(jnp.int32, (rt_ref.shape[0], ring * padded), 1)
-    same = (out_row // ring == in_row % padded) & (out_row % ring == in_row // padded) & (out_row < terms * ring)
+    block = back[:rows] + back[rows : 2 * rows]
+    most = jnp.max(jnp.abs(block), axis=0, keepdims=True)
+    scale = (most * (1.01 / 32767)).astype(BF16).astype(F32)
+    inverse = jnp.where(scale > 0, 1.0 / jnp.where(scale > 0, scale, 1.0), 0.0)
+    hl[e] = jnp.round(block * inverse).astype(jnp.int32).astype(jnp.int16)
+    wide = cols // 128
+    used_rows = wide * (terms - main)
+    tail = jnp.concatenate(
+        [rrow[pl.ds(main + n // wide, 1), (n % wide) * 128 : (n % wide + 1) * 128] for n in range(used_rows)]
+        + [scale[:, n * 128 : (n + 1) * 128] for n in range(wide)]
+        + [jnp.zeros((16 - used_rows - wide, 128), F32)],
+        axis=0,
+    )
+    rg_last[e] = tail.astype(BF16)
+
+    for h in range(last_step):
+        move(psi_chains, h)
+        move(right_chains, h + 1)
+
+    out_row = lax.broadcasted_iota(jnp.int32, (main * ring, ring * main), 0)
+    in_row = lax.broadcasted_iota(jnp.int32, (main * ring, ring * main), 1)
+    same = (out_row // ring == in_row % main) & (out_row % ring == in_row // main)
     order = jnp.where(same, 1.0, 0.0).astype(BF16)
-    rt_ref[...] = jnp.dot(order, rg[...].reshape(ring * padded, cols), preferred_element_type=F32).astype(BF16)
-
+    rt_ref[: main * ring] = jnp.dot(
+        order, rg[...].reshape(ring * main, cols), preferred_element_type=F32
+    ).astype(BF16)
+
+    move(psi_chains, last_step)
     loads[5].wait()
-    for n in range(psi_parts):
-        forward(hl, 0, n, steps)
-    block = cols // 2
     lanes = q_ref.shape[3]
     lhs = left_ref[...].reshape(terms * rows, cols)
-    for half in range(2):
-        x_high = hl[:, :rows, half * block : (half + 1) * block].reshape(ring * rows, block)
-        x_low = hl[:, rows:, half * block : (half + 1) * block].reshape(ring * rows, block)
-        q = jnp.dot(lhs, x_high, preferred_element_type=F32) + jnp.dot(lhs, x_low, preferred_element_type=F32)
-        for part in range(block // lanes):
-            q_ref[:, half * (block // lanes) + part] = q[:, part * lanes : (part + 1) * lanes].reshape(
-                terms, rows, lanes
+    block = 2 * lanes
+    for half in range(cols // block):
+        high, low = [], []
+        for k in range(ring):
+            tail = rg_last[k].astype(F32)
+            scale = jnp.concatenate(
+                [tail[used_rows + 2 * half + n : used_rows + 2 * half + n + 1] for n in range(2)], axis=1
             )
+            x = hl[k, :, half * block : (half + 1) * block].astype(jnp.int32).astype(F32) * scale
+            high.append(x.astype(BF16))
+            low.append((x - high[-1].astype(F32)).astype(BF16))
+        q = jnp.dot(lhs, jnp.concatenate(high, axis=0), preferred_element_type=F32) + jnp.dot(
+            lhs, jnp.concatenate(low, axis=0), preferred_element_type=F32
+        )
+        for part in range(2):
+            q_ref[:, half * 2 + part] = q[:, part * lanes : (part + 1) * lanes].reshape(terms, rows, lanes)
+
+    last = rt_ref.shape[0] - main * ring
+    out_row = lax.broadcasted_iota(jnp.int32, (last, ring * 16), 0)
+    in_row = lax.broadcasted_iota(jnp.int32, (last, ring * 16), 1)
+    for n in range(wide):
+        same = (out_row % ring == in_row // 16) & ((out_row // ring) * wide + n == in_row % 16) & (in_row % 16 < used_rows)
+        order = jnp.where(same, 1.0, 0.0).astype(BF16)
+        rt_ref[main * ring :, n * 128 : (n + 1) * 128] = jnp.dot(
+            order, rg_last[...].reshape(ring * 16, 128), preferred_element_type=F32
+        ).astype(BF16)
 
     for copy in spread:
         copy.wait_send()
@@ -304,8 +348,9 @@
             pltpu.VMEM((cols, 128), F32),
             pltpu.VMEM((groups, per, 128), BF16),
             pltpu.VMEM((groups, per, 128), BF16),
-            pltpu.VMEM((ring, 2 * rows, cols), BF16),
-            pltpu.VMEM((ring, padded, cols), BF16),
+            pltpu.VMEM((ring, rows, cols), jnp.int16),
+            pltpu.VMEM((ring, terms // 16 * 16, cols), BF16),
+            pltpu.VMEM((ring, 16, 128), BF16),
             pltpu.VMEM((padded, cols), F32),
             sems((groups,)),
             sems((groups,)),

time: 76.2 us -> 70.4 us (0.924)
  Pallas kernels: 75.4 us -> 69.6 us
    pallas_call x1, Pallas kernels: 45.5 us -> 42.3 us  [body(): pl.pallas_call(functools.partial(gather_kernel, groups, ring), out_shape=...]
    pallas_call x1, Pallas kernels: 22.5 us -> 19.8 us  [body(): pl.pallas_call(scatter_kernel, out_shape=jax.ShapeDtypeStruct((1, rows, c...]
where the time goes in v3:
time: 70.4 us; the launch traced here: 70.2 us
  Pallas kernels  69.6 us (99%)
    pallas_call x1, Pallas kernels, body(): pl.pallas_call(functools.partial(gather_kernel, groups, ring), out_shape=...  42.3 us
    pallas_call x1, Pallas kernels, body(): pl.pallas_call(scatter_kernel, out_shape=jax.ShapeDtypeStruct((1, rows, c...  19.8 us
    pallas_call x1, Pallas kernels, body(): pl.pallas_call(functools.partial(combine_kernel, 16), out_shape=(sums, su...  7.4 us

profile of v3, /device:TPU:1, one launch (start us, length us, event | category | flops | bytes accessed | tf_op | source)
XLA Modules:
  0.0 70.2 jit_solution(16454186961228319889)
XLA Ops:
  0.0 42.3 %gather_psi.1 = (f32[34,4,32,128]{3,2,1,0:T(8,128)S(1)}, bf16[640,512]{1,0:T(8,128)(2,1)S(1)}, s32[4,128]{1,0:T(4,128)S(1)}) custom-call(f32[1,32,512]{2,1,0:T(8,128)} %psi_hbm.1, bf16[34,32,512]{2,1,0:T(8,128)(2,1)} %left_hbm.1, bf16[34,32,512]{2,1,0:T(8,128)(2,1)} %right_hbm.1, s32[4,128]{1,0:T(4,128)} %bitcast.9, s32[4,128]{1,0:T(4,128)} %bitcast.10, ...), custom_call_target="tpu_custom_call" | custom-call | tf_op jit(solution)/shard_map/gather_psi/pallas_call | solution.py:334
  42.3 7.4 %combine_tasks.1 = (f32[160,4,8,128]{3,2,1,0:T(8,128)S(1)}, f32[160,4,8,128]{3,2,1,0:T(8,128)S(1)}) custom-call(f32[136,4,8,128]{3,2,1,0:T(8,128)S(1)} %bitcast.8, s32[4,128]{1,0:T(4,128)S(1)} %get-tuple-element.11.pk_ref), custom_call_target="tpu_custom_call" | custom-call | tf_op jit(solution)/shard_map/combine_tasks/pallas_call | solution.py:369
  49.8 19.8 %scatter_sums.1 = f32[1,32,512]{2,1,0:T(8,128)S(1)} custom-call(f32[16,2,5,32,128]{4,3,2,1,0:T(8,128)S(1)} %bitcast.6, f32[16,2,5,32,128]{4,3,2,1,0:T(8,128)S(1)} %bitcast.7, bf16[640,512]{1,0:T(8,128)(2,1)S(1)} %get-tuple-element.14.rt_ref), custom_call_target="tpu_custom_call" | custom-call | tf_op jit(solution)/shard_map/scatter_sums/pallas_call | solution.py:380
  69.6 0.6 copy.8

commit v4 on v3

--- a/solution.py
+++ b/solution.py
@@ -17,7 +17,7 @@
 
 
 def gather_kernel(groups, ring, psi_hbm, left_hbm, right_hbm, in_hbm, out_hbm, term_hbm, q_ref, rt_ref, pk_ref,
-                  psi_ref, left_ref, right_ref, ids, t_scr, send_buf, got, hl, rg, rg_last, rrow,
+                  psi_ref, left_ref, right_ref, ids, t_scr, send_buf, got, hl, rg, rg_last, rrow, xh, xl,
                   a_send, a_recv, z_send, z_recv, local):
     g = lax.axis_index("sec")
     e = lax.axis_index("env")
@@ -138,8 +138,8 @@
     pk_ref[...] = (
         w * 4 + (s >> 3)
         + ((r * (rt_ref.shape[0] // 128) + (w >> 3)) << 8)
-        + (((w - s) & 7) << 16)
-        + ((w & 7) << 20)
+        + ((((w - s) & 7) * (128 // 8)) << 16)
+        + ((w & 7) << 24)
     )
 
     for copy in spread:
@@ -160,9 +160,23 @@
     )
     rg_last[e] = tail.astype(BF16)
 
+    def unpack(off):
+        slot = lax.rem(e + off + ring, ring)
+        tail = rg_last[slot].astype(F32)
+        scale = jnp.concatenate([tail[used_rows + n : used_rows + n + 1] for n in range(wide)], axis=1)
+        x = hl[slot].astype(jnp.int32).astype(F32) * scale
+        high = x.astype(BF16)
+        xh[slot] = high
+        xl[slot] = (x - high.astype(F32)).astype(BF16)
+
+    there = [[0]] + [[] for _ in range(last_step)]
+    for h in range(last_step):
+        there[h + 1] += [-jump - h] + [jump + h] * (h < steps - jump) + [-1 - h, 1 + h] * (h < jump - 1)
     for h in range(last_step):
         move(psi_chains, h)
         move(right_chains, h + 1)
+        for off in there[h]:
+            unpack(off)
 
     out_row = lax.broadcasted_iota(jnp.int32, (main * ring, ring * main), 0)
     in_row = lax.broadcasted_iota(jnp.int32, (main * ring, ring * main), 1)
@@ -173,22 +187,16 @@
     ).astype(BF16)
 
     move(psi_chains, last_step)
+    for off in there[last_step]:
+        unpack(off)
     loads[5].wait()
     lanes = q_ref.shape[3]
     lhs = left_ref[...].reshape(terms * rows, cols)
     block = 2 * lanes
     for half in range(cols // block):
-        high, low = [], []
-        for k in range(ring):
-            tail = rg_last[k].astype(F32)
-            scale = jnp.concatenate(
-                [tail[used_rows + 2 * half + n : used_rows + 2 * half + n + 1] for n in range(2)], axis=1
-            )
-            x = hl[k, :, half * block : (half + 1) * block].astype(jnp.int32).astype(F32) * scale
-            high.append(x.astype(BF16))
-            low.append((x - high[-1].astype(F32)).astype(BF16))
-        q = jnp.dot(lhs, jnp.concatenate(high, axis=0), preferred_element_type=F32) + jnp.dot(
-            lhs, jnp.concatenate(low, axis=0), preferred_element_type=F32
+        at = slice(half * block, (half + 1) * block)
+        q = jnp.dot(lhs, xh[:, :, at].reshape(ring * rows, block), preferred_element_type=F32) + jnp.dot(
+            lhs, xl[:, :, at].reshape(ring * rows, block), preferred_element_type=F32
         )
         for part in range(2):
             q_ref[:, half * 2 + part] = q[:, part * lanes : (part + 1) * lanes].reshape(terms, rows, lanes)
@@ -210,7 +218,6 @@
 
 
 def combine_kernel(unroll, q_ref, pk_ref, b0_ref, b1_ref):
-    tasks = pk_ref.shape[0] * pk_ref.shape[1]
     lanes = q_ref.shape[-1]
     per = lanes // 8
     b0_ref[...] = jnp.zeros_like(b0_ref)
@@ -218,23 +225,23 @@
     shape = q_ref.shape[1:]
     group = lax.broadcasted_iota(jnp.int32, shape, 2) // per
 
-    def step(n, carry):
+    def step(line, n, carry):
         moved = []
         for u in range(unroll):
-            t = n * unroll + u
-            word = pk_ref[t // 128, t % 128]
+            word = pk_ref[line, n * unroll + u]
             block = q_ref[word & 255].reshape(shape[0] * shape[1], lanes)
-            block = pltpu.roll(block, ((word >> 16) & 15) * per, axis=1).reshape(shape)
-            moved.append(((word >> 8) & 255, jnp.where(group == (word >> 20), block, 0.0)))
+            block = pltpu.roll(block, (word >> 16) & 127, axis=1).reshape(shape)
+            moved.append(((word >> 8) & 255, jnp.where(group == (word >> 24), block, 0.0)))
         for u, (place, block) in enumerate(moved):
             b_ref = (b0_ref, b1_ref)[u % 2]
             b_ref[place] = b_ref[place] + block
         return carry
 
-    lax.fori_loop(0, tasks // unroll, step, 0)
-
-
-def scatter_kernel(b0_ref, b1_ref, rt_ref, o_ref, mine, pair, acc, xa, yb, ca, cb, ya, xb, send, recv):
+    for line in range(pk_ref.shape[0]):
+        lax.fori_loop(0, pk_ref.shape[1] // unroll, functools.partial(step, line), 0)
+
+
+def scatter_kernel(b0_ref, b1_ref, rt_ref, o_ref, mine, pair, acc, coded, steps, xa, yb, xs, ys, ca, cb, ya, xb, send, recv):
     g = lax.axis_index("sec")
     core = lax.rem(g, 2)
     x = lax.rem(g // 2, 4)
@@ -278,7 +285,12 @@
         made.start()
         return made
 
-    first, second, third = [], [], []
+    steps[...] = jnp.zeros_like(steps)
+    first, second, scales, third = [], [], [], []
+
+    def decoded(values, scale):
+        return [values[n].astype(jnp.int32).astype(F32) * scale[n : n + 1, :1] for n in range(4)]
+
     for k in range(2):
         mine[k] = product(1 - core, k).reshape(mine.shape[1:])
         if k == 0:
@@ -288,19 +300,39 @@
         own = product(core, k).reshape(acc.shape[1:])
         first[k].wait_recv()
         acc[k] = own + pair[k].reshape(acc.shape[1:])
+        for n in range(16):
+            part = acc[k, n // 4, n % 4]
+            most = jnp.max(jnp.max(jnp.abs(part), axis=0, keepdims=True), axis=1, keepdims=True)
+            scale = most * (1.01 / 32767)
+            inverse = jnp.where(scale > 0, 1.0 / jnp.where(scale > 0, scale, 1.0), 0.0)
+            coded[k, n // 4, n % 4] = jnp.round(part * inverse).astype(jnp.int32).astype(jnp.int16)
+            wide = jnp.broadcast_to(scale, (1, 128))
+            if k == 0:
+                steps[k, n % 4, pl.ds(n // 4, 1), :] = wide
+            else:
+                steps[k, n // 4, pl.ds(n % 4, 1), :] = wide
         for d in (2, 1, 3):
             index = 2 + k * 3 + d - 1
             if k == 0:
-                second.append(copy(acc.at[0, :, lax.rem(x + d, 4)], xa.at[d - 1], index, x_peer(d)))
+                to = lax.rem(x + d, 4)
+                second.append(copy(coded.at[0, :, to], xa.at[d - 1], index, x_peer(d)))
+                scales.append(copy(steps.at[0, to], xs.at[d - 1], index + 12, x_peer(d)))
             else:
-                second.append(copy(acc.at[1, lax.rem(y + d, 4)], yb.at[d - 1], index, y_peer(d)))
+                to = lax.rem(y + d, 4)
+                second.append(copy(coded.at[1, to], yb.at[d - 1], index, y_peer(d)))
+                scales.append(copy(steps.at[1, to], ys.at[d - 1], index + 12, y_peer(d)))
     for k in range(2):
         for d in (1, 2, 3):
             second[k * 3 + d - 1].wait_recv()
+            scales[k * 3 + d - 1].wait_recv()
         if k == 0:
-            ca[...] = acc[0, :, x] + xa[0] + xa[1] + xa[2]
+            parts = [decoded(xa[d], xs[d]) for d in range(3)]
+            for n in range(4):
+                ca[n] = acc[0, n, x] + parts[0][n] + parts[1][n] + parts[2][n]
         else:
-            cb[...] = acc[1, y] + yb[0] + yb[1] + yb[2]
+            parts = [decoded(yb[d], ys[d]) for d in range(3)]
+            for n in range(4):
+                cb[n] = acc[1, y, n] + parts[0][n] + parts[1][n] + parts[2][n]
         for d in (2, 1, 3):
             index = 8 + k * 3 + d - 1
             if k == 0:
@@ -314,7 +346,7 @@
             o_ref[0, :half] = ca[y] + ya[0] + ya[1] + ya[2]
         else:
             o_ref[0, half:] = cb[x] + xb[0] + xb[1] + xb[2]
-    for made in first + second + third:
+    for made in first + second + scales + third:
         made.wait_send()
 
 
@@ -352,6 +384,8 @@
             pltpu.VMEM((ring, terms // 16 * 16, cols), BF16),
             pltpu.VMEM((ring, 16, 128), BF16),
             pltpu.VMEM((padded, cols), F32),
+            pltpu.VMEM((ring, rows, cols), BF16),
+            pltpu.VMEM((ring, rows, cols), BF16),
             sems((groups,)),
             sems((groups,)),
             sems((8 * ring,)),
@@ -386,14 +420,18 @@
             pltpu.VMEM((2, 16, half, cols), F32),
             pltpu.VMEM((2, 16, half, cols), F32),
             pltpu.VMEM((2, 4, 4, half, cols), F32),
-            pltpu.VMEM((3, 4, half, cols), F32),
-            pltpu.VMEM((3, 4, half, cols), F32),
+            pltpu.VMEM((2, 4, 4, half, cols), jnp.int16),
+            pltpu.VMEM((2, 4, 8, 128), F32),
+            pltpu.VMEM((3, 4, half, cols), jnp.int16),
+            pltpu.VMEM((3, 4, half, cols), jnp.int16),
+            pltpu.VMEM((3, 8, 128), F32),
+            pltpu.VMEM((3, 8, 128), F32),
             pltpu.VMEM((4, half, cols), F32),
             pltpu.VMEM((4, half, cols), F32),
             pltpu.VMEM((3, half, cols), F32),
             pltpu.VMEM((3, half, cols), F32),
-            sems((14,)),
-            sems((14,)),
+            sems((20,)),
+            sems((20,)),
         ],
         compiler_params=pltpu.CompilerParams(collective_id=1, has_side_effects=True, vmem_limit_bytes=limit),
         name="scatter_sums",

time: 70.4 us -> 66.2 us (0.940)
  Pallas kernels: 69.6 us -> 65.4 us
    pallas_call x1, Pallas kernels: 7.4 us -> 5.29 us  [body(): pl.pallas_call(functools.partial(combine_kernel, 16), out_shape=(sums, su...]
    pallas_call x1, Pallas kernels: 19.8 us -> 17.8 us  [body(): pl.pallas_call(scatter_kernel, out_shape=jax.ShapeDtypeStruct((1, rows, c...]
where the time goes in v4:
time: 66.2 us; the launch traced here: 66 us
  Pallas kernels  65.4 us (99%)
    pallas_call x1, Pallas kernels, body(): pl.pallas_call(functools.partial(gather_kernel, groups, ring), out_shape=...  42.3 us
    pallas_call x1, Pallas kernels, body(): pl.pallas_call(scatter_kernel, out_shape=jax.ShapeDtypeStruct((1, rows, c...  17.8 us
    pallas_call x1, Pallas kernels, body(): pl.pallas_call(functools.partial(combine_kernel, 16), out_shape=(sums, su...  5.29 us

profile of v4, /device:TPU:1, one launch (start us, length us, event | category | flops | bytes accessed | tf_op | source)
XLA Modules:
  0.0 66.0 jit_solution(17042656640355885952)
XLA Ops:
  0.0 42.3 %gather_psi.1 = (f32[34,4,32,128]{3,2,1,0:T(8,128)S(1)}, bf16[640,512]{1,0:T(8,128)(2,1)S(1)}, s32[4,128]{1,0:T(4,128)S(1)}) custom-call(f32[1,32,512]{2,1,0:T(8,128)} %psi_hbm.1, bf16[34,32,512]{2,1,0:T(8,128)(2,1)} %left_hbm.1, bf16[34,32,512]{2,1,0:T(8,128)(2,1)} %right_hbm.1, s32[4,128]{1,0:T(4,128)} %bitcast.9, s32[4,128]{1,0:T(4,128)} %bitcast.10, ...), custom_call_target="tpu_custom_call" | custom-call | tf_op jit(solution)/shard_map/gather_psi/pallas_call | solution.py:366
  42.3 5.3 %combine_tasks.1 = (f32[160,4,8,128]{3,2,1,0:T(8,128)S(1)}, f32[160,4,8,128]{3,2,1,0:T(8,128)S(1)}) custom-call(f32[136,4,8,128]{3,2,1,0:T(8,128)S(1)} %bitcast.8, s32[4,128]{1,0:T(4,128)S(1)} %get-tuple-element.11.pk_ref), custom_call_target="tpu_custom_call" | custom-call | tf_op jit(solution)/shard_map/combine_tasks/pallas_call | solution.py:403
  47.6 17.8 %scatter_sums.1 = f32[1,32,512]{2,1,0:T(8,128)S(1)} custom-call(f32[16,2,5,32,128]{4,3,2,1,0:T(8,128)S(1)} %bitcast.6, f32[16,2,5,32,128]{4,3,2,1,0:T(8,128)S(1)} %bitcast.7, bf16[640,512]{1,0:T(8,128)(2,1)S(1)} %get-tuple-element.14.rt_ref), custom_call_target="tpu_custom_call" | custom-call | tf_op jit(solution)/shard_map/scatter_sums/pallas_call | solution.py:414
  65.4 0.6 copy.8

commit v5 on v4

--- a/solution.py
+++ b/solution.py
@@ -27,9 +27,10 @@
     per = cols // groups
     right = lax.rem(e + 1, ring)
     left = lax.rem(e + ring - 1, ring)
-    jump = ring // 4
-    far_right = lax.rem(e + jump, ring)
-    far_left = lax.rem(e + ring - jump, ring)
+    steps = ring // 2
+    psi_starts = (1, 5)
+    right_starts = (1, 5)
+    leaps = sorted({1, *psi_starts, *right_starts})
 
     loads = [
         pltpu.make_async_copy(src, dst, local.at[n])
@@ -50,7 +51,7 @@
     barrier = pltpu.get_barrier_semaphore()
     for d in range(1, groups):
         pl.semaphore_signal(barrier, inc=1, device_id={"sec": lax.rem(g + d, groups)}, device_id_type=MESH)
-    for to in (left, right, far_left, far_right):
+    for to in [lax.rem(e + leap, ring) for leap in (*leaps, *(ring - leap for leap in leaps))]:
         pl.semaphore_signal(barrier, inc=1, device_id={"env": to}, device_id_type=MESH)
 
     loads[0].wait()
@@ -64,7 +65,7 @@
     for p in range(groups):
         send_buf[p] = t_scr[pl.ds(p, per, stride=groups), :].astype(BF16)
 
-    pl.semaphore_wait(barrier, groups + 3)
+    pl.semaphore_wait(barrier, groups - 1 + 2 * len(leaps))
 
     spread = []
     for d in range(1, groups):
@@ -90,12 +91,11 @@
         rrow[pl.ds(w, 1), :] = row
     rg[e] = rrow[:main].astype(BF16)
 
-    steps = ring // 2
     flights = {}
     used = []
 
     def forward(chain, h):
-        key, buffer, hops, place = chain
+        key, buffer, hops, place, _ = chain
         if (key, h - 1) in flights:
             flights[key, h - 1].wait_recv()
         if h < hops:
@@ -114,17 +114,26 @@
             copy.start()
             flights[key, h] = copy
 
-    def chains(key, buffer):
-        return (
-            (key + "br", buffer, steps - jump + 1, lambda h: (1 - jump - h, right) if h else (0, far_right)),
-            (key + "bl", buffer, steps - jump, lambda h: (jump - 1 + h, left) if h else (0, far_left)),
-            (key + "ar", buffer, jump - 1, lambda h: (-h, right)),
-            (key + "al", buffer, jump - 1, lambda h: (h, left)),
-        )
-
-    psi_chains = chains("p", hl) + chains("t", rg_last)
-    right_chains = chains("m", rg)
-    last_step = steps - jump + 1
+    def chains(key, buffer, starts):
+        made = []
+        for n in range(len(starts) - 1, -1, -1):
+            o = starts[n]
+            for sign, end in ((1, steps + 1), (-1, steps)):
+                stop = min(starts[n + 1], end) if n + 1 < len(starts) else end
+                beside = right if sign > 0 else left
+                seed = lax.rem(e + sign * o + ring, ring)
+                place = functools.partial(
+                    lambda sign, o, seed, beside, h: (-sign * (o + h - 1), beside) if h else (0, seed),
+                    sign, o, seed, beside,
+                )
+                made.append((key + str(sign * o), buffer, stop - o, place, [-sign * k for k in range(o, stop)]))
+        return made
+
+    psi_chains = chains("p", hl, psi_starts)
+    tail_chains = chains("t", rg_last, psi_starts)
+    right_chains = chains("m", rg, right_starts)
+    last_step = max(chain[2] for chain in psi_chains)
+    right_last = max(chain[2] for chain in right_chains)
 
     def move(group, h):
         for chain in group:
@@ -170,13 +179,22 @@
         xl[slot] = (x - high.astype(F32)).astype(BF16)
 
     there = [[0]] + [[] for _ in range(last_step)]
-    for h in range(last_step):
-        there[h + 1] += [-jump - h] + [jump + h] * (h < steps - jump) + [-1 - h, 1 + h] * (h < jump - 1)
-    for h in range(last_step):
-        move(psi_chains, h)
+    for chain in psi_chains:
+        for h, off in enumerate(chain[4]):
+            there[h + 1].append(off)
+    for h in range(max(last_step, right_last)):
+        if h < last_step:
+            move(psi_chains + tail_chains, h)
         move(right_chains, h + 1)
-        for off in there[h]:
-            unpack(off)
+        if h < last_step:
+            for off in there[h]:
+                unpack(off)
+        if h == 0:
+            for copy in spread:
+                copy.wait_send()
+        for (key, at), copy in flights.items():
+            if at == h - 1:
+                copy.wait_send()
 
     out_row = lax.broadcasted_iota(jnp.int32, (main * ring, ring * main), 0)
     in_row = lax.broadcasted_iota(jnp.int32, (main * ring, ring * main), 1)
@@ -186,7 +204,7 @@
         order, rg[...].reshape(ring * main, cols), preferred_element_type=F32
     ).astype(BF16)
 
-    move(psi_chains, last_step)
+    move(psi_chains + tail_chains, last_step)
     for off in there[last_step]:
         unpack(off)
     loads[5].wait()
@@ -211,10 +229,9 @@
             order, rg_last[...].reshape(ring * 16, 128), preferred_element_type=F32
         ).astype(BF16)
 
-    for copy in spread:
-        copy.wait_send()
-    for copy in flights.values():
-        copy.wait_send()
+    for (key, at), copy in flights.items():
+        if at >= max(last_step, right_last) - 1:
+            copy.wait_send()
 
 
 def combine_kernel(unroll, q_ref, pk_ref, b0_ref, b1_ref):
@@ -401,7 +418,7 @@
 
     sums = jax.ShapeDtypeStruct((groups * tiles, rows // 8, 8, 128), F32)
     even, odd = pl.pallas_call(
-        functools.partial(combine_kernel, 16),
+        functools.partial(combine_kernel, 128),
         out_shape=(sums, sums),
         in_specs=[vmem(), pl.BlockSpec(memory_space=pltpu.SMEM)],
         out_specs=(vmem(), vmem()),

time: 66.2 us -> 63.6 us (0.961)
  Pallas kernels: 65.4 us -> 62.8 us
    pallas_call x1, Pallas kernels: 5.29 us -> 3.07 us  [body(): pl.pallas_call(functools.partial(combine_kernel, 128), out_shape=(sums, s...]
where the time goes in v5:
time: 63.6 us; the launch traced here: 63.5 us
  Pallas kernels  62.8 us (99%)
    pallas_call x1, Pallas kernels, body(): pl.pallas_call(functools.partial(gather_kernel, groups, ring), out_shape=...  41.7 us
    pallas_call x1, Pallas kernels, body(): pl.pallas_call(scatter_kernel, out_shape=jax.ShapeDtypeStruct((1, rows, c...  18 us
    pallas_call x1, Pallas kernels, body(): pl.pallas_call(functools.partial(combine_kernel, 128), out_shape=(sums, s...  3.07 us

profile of v5, /device:TPU:1, one launch (start us, length us, event | category | flops | bytes accessed | tf_op | source)
XLA Modules:
  0.0 63.5 jit_solution(18067560008747693760)
XLA Ops:
  0.0 41.7 %gather_psi.1 = (f32[34,4,32,128]{3,2,1,0:T(8,128)S(1)}, bf16[640,512]{1,0:T(8,128)(2,1)S(1)}, s32[4,128]{1,0:T(4,128)S(1)}) custom-call(f32[1,32,512]{2,1,0:T(8,128)} %psi_hbm.1, bf16[34,32,512]{2,1,0:T(8,128)(2,1)} %left_hbm.1, bf16[34,32,512]{2,1,0:T(8,128)(2,1)} %right_hbm.1, s32[4,128]{1,0:T(4,128)} %bitcast.9, s32[4,128]{1,0:T(4,128)} %bitcast.10, ...), custom_call_target="tpu_custom_call" | custom-call | tf_op jit(solution)/shard_map/gather_psi/pallas_call | solution.py:383
  41.7 3.1 %combine_tasks.1 = (f32[160,4,8,128]{3,2,1,0:T(8,128)S(1)}, f32[160,4,8,128]{3,2,1,0:T(8,128)S(1)}) custom-call(f32[136,4,8,128]{3,2,1,0:T(8,128)S(1)} %bitcast.8, s32[4,128]{1,0:T(4,128)S(1)} %get-tuple-element.11.pk_ref), custom_call_target="tpu_custom_call" | custom-call | tf_op jit(solution)/shard_map/combine_tasks/pallas_call | solution.py:420
  44.8 18.0 %scatter_sums.1 = f32[1,32,512]{2,1,0:T(8,128)S(1)} custom-call(f32[16,2,5,32,128]{4,3,2,1,0:T(8,128)S(1)} %bitcast.6, f32[16,2,5,32,128]{4,3,2,1,0:T(8,128)S(1)} %bitcast.7, bf16[640,512]{1,0:T(8,128)(2,1)S(1)} %get-tuple-element.14.rt_ref), custom_call_target="tpu_custom_call" | custom-call | tf_op jit(solution)/shard_map/scatter_sums/pallas_call | solution.py:431
  62.8 0.6 copy.8

commit v6 on v5

--- a/solution.py
+++ b/solution.py
@@ -258,7 +258,7 @@
         lax.fori_loop(0, pk_ref.shape[1] // unroll, functools.partial(step, line), 0)
 
 
-def scatter_kernel(b0_ref, b1_ref, rt_ref, o_ref, mine, pair, acc, coded, steps, xa, yb, xs, ys, ca, cb, ya, xb, send, recv):
+def scatter_kernel(b0_ref, b1_ref, rt_ref, o_ref, mine, pair, mine_steps, pair_steps, acc, coded, steps, xa, yb, xs, ys, ca, cb, ya, xb, send, recv):
     g = lax.axis_index("sec")
     core = lax.rem(g, 2)
     x = lax.rem(g // 2, 4)
@@ -305,24 +305,34 @@
     steps[...] = jnp.zeros_like(steps)
     first, second, scales, third = [], [], [], []
 
+    def code(part):
+        most = jnp.max(jnp.max(jnp.abs(part), axis=0, keepdims=True), axis=1, keepdims=True)
+        scale = most * (1.01 / 32767)
+        inverse = jnp.where(scale > 0, 1.0 / jnp.where(scale > 0, scale, 1.0), 0.0)
+        return scale, jnp.round(part * inverse).astype(jnp.int32).astype(jnp.int16)
+
     def decoded(values, scale):
         return [values[n].astype(jnp.int32).astype(F32) * scale[n : n + 1, :1] for n in range(4)]
 
     for k in range(2):
-        mine[k] = product(1 - core, k).reshape(mine.shape[1:])
+        theirs = product(1 - core, k).reshape(mine.shape[1:])
+        for n in range(16):
+            scale, mine[k, n] = code(theirs[n])
+            mine_steps[k, pl.ds(n, 1), :] = jnp.broadcast_to(scale, (1, 128))
         if k == 0:
             pl.semaphore_wait(barrier, len(peers))
         first.append(copy(mine.at[k], pair.at[k], k, sibling))
+        scales.append(copy(mine_steps.at[k], pair_steps.at[k], 20 + k, sibling))
     for k in range(2):
-        own = product(core, k).reshape(acc.shape[1:])
+        own = product(core, k).reshape(mine.shape[1:])
         first[k].wait_recv()
-        acc[k] = own + pair[k].reshape(acc.shape[1:])
+        scales[k].wait_recv()
+        for n in range(16):
+            arrived = pair[k, n].astype(jnp.int32).astype(F32) * pair_steps[k, n : n + 1, :1]
+            acc[k, n // 4, n % 4] = own[n] + arrived
         for n in range(16):
             part = acc[k, n // 4, n % 4]
-            most = jnp.max(jnp.max(jnp.abs(part), axis=0, keepdims=True), axis=1, keepdims=True)
-            scale = most * (1.01 / 32767)
-            inverse = jnp.where(scale > 0, 1.0 / jnp.where(scale > 0, scale, 1.0), 0.0)
-            coded[k, n // 4, n % 4] = jnp.round(part * inverse).astype(jnp.int32).astype(jnp.int16)
+            scale, coded[k, n // 4, n % 4] = code(part)
             wide = jnp.broadcast_to(scale, (1, 128))
             if k == 0:
                 steps[k, n % 4, pl.ds(n // 4, 1), :] = wide
@@ -341,7 +351,7 @@
     for k in range(2):
         for d in (1, 2, 3):
             second[k * 3 + d - 1].wait_recv()
-            scales[k * 3 + d - 1].wait_recv()
+            scales[2 + k * 3 + d - 1].wait_recv()
         if k == 0:
             parts = [decoded(xa[d], xs[d]) for d in range(3)]
             for n in range(4):
@@ -434,8 +444,10 @@
         in_specs=[vmem()] * 3,
         out_specs=vmem(),
         scratch_shapes=[
-            pltpu.VMEM((2, 16, half, cols), F32),
-            pltpu.VMEM((2, 16, half, cols), F32),
+            pltpu.VMEM((2, 16, half, cols), jnp.int16),
+            pltpu.VMEM((2, 16, half, cols), jnp.int16),
+            pltpu.VMEM((2, 16, 128), F32),
+            pltpu.VMEM((2, 16, 128), F32),
             pltpu.VMEM((2, 4, 4, half, cols), F32),
             pltpu.VMEM((2, 4, 4, half, cols), jnp.int16),
             pltpu.VMEM((2, 4, 8, 128), F32),
@@ -447,8 +459,8 @@
             pltpu.VMEM((4, half, cols), F32),
             pltpu.VMEM((3, half, cols), F32),
             pltpu.VMEM((3, half, cols), F32),
-            sems((20,)),
-            sems((20,)),
+            sems((22,)),
+            sems((22,)),
         ],
         compiler_params=pltpu.CompilerParams(collective_id=1, has_side_effects=True, vmem_limit_bytes=limit),
         name="scatter_sums",

time: 63.6 us -> 62.7 us (0.986)
  Pallas kernels: 62.8 us -> 61.9 us
    pallas_call x1, Pallas kernels: 18 us -> 17.2 us  [body(): pl.pallas_call(scatter_kernel, out_shape=jax.ShapeDtypeStruct((1, rows, c...]
where the time goes in v6:
time: 62.7 us; the launch traced here: 62.6 us
  Pallas kernels  61.9 us (99%)
  local copies, waits for them, and re-layouts  0.63 us (1%)
    pallas_call x1, Pallas kernels, body(): pl.pallas_call(functools.partial(gather_kernel, groups, ring), out_shape=...  41.7 us
    pallas_call x1, Pallas kernels, body(): pl.pallas_call(scatter_kernel, out_shape=jax.ShapeDtypeStruct((1, rows, c...  17.2 us
    pallas_call x1, Pallas kernels, body(): pl.pallas_call(functools.partial(combine_kernel, 128), out_shape=(sums, s...  3.07 us

profile of v6, /device:TPU:1, one launch (start us, length us, event | category | flops | bytes accessed | tf_op | source)
XLA Modules:
  0.0 62.6 jit_solution(9135546361994799849)
XLA Ops:
  0.0 41.7 %gather_psi.1 = (f32[34,4,32,128]{3,2,1,0:T(8,128)S(1)}, bf16[640,512]{1,0:T(8,128)(2,1)S(1)}, s32[4,128]{1,0:T(4,128)S(1)}) custom-call(f32[1,32,512]{2,1,0:T(8,128)} %psi_hbm.1, bf16[34,32,512]{2,1,0:T(8,128)(2,1)} %left_hbm.1, bf16[34,32,512]{2,1,0:T(8,128)(2,1)} %right_hbm.1, s32[4,128]{1,0:T(4,128)} %bitcast.9, s32[4,128]{1,0:T(4,128)} %bitcast.10, ...), custom_call_target="tpu_custom_call" | custom-call | tf_op jit(solution)/shard_map/gather_psi/pallas_call | solution.py:393
  41.7 3.1 %combine_tasks.1 = (f32[160,4,8,128]{3,2,1,0:T(8,128)S(1)}, f32[160,4,8,128]{3,2,1,0:T(8,128)S(1)}) custom-call(f32[136,4,8,128]{3,2,1,0:T(8,128)S(1)} %bitcast.8, s32[4,128]{1,0:T(4,128)S(1)} %get-tuple-element.11.pk_ref), custom_call_target="tpu_custom_call" | custom-call | tf_op jit(solution)/shard_map/combine_tasks/pallas_call | solution.py:430
  44.8 17.2 %scatter_sums.1 = f32[1,32,512]{2,1,0:T(8,128)S(1)} custom-call(f32[16,2,5,32,128]{4,3,2,1,0:T(8,128)S(1)} %bitcast.6, f32[16,2,5,32,128]{4,3,2,1,0:T(8,128)S(1)} %bitcast.7, bf16[640,512]{1,0:T(8,128)(2,1)S(1)} %get-tuple-element.14.rt_ref), custom_call_target="tpu_custom_call" | custom-call | tf_op jit(solution)/shard_map/scatter_sums/pallas_call | solution.py:441
  62.0 0.6 %copy.8 = f32[1,32,512]{2,1,0:T(8,128)} copy(f32[1,32,512]{2,1,0:T(8,128)S(1)} %scatter_sums.1) | data formatting | bytes 131072

commit v7 on v6

--- a/solution.py
+++ b/solution.py
@@ -62,14 +62,13 @@
         [high.astype(F32), low.astype(F32), jnp.zeros((128 - 2 * rows, cols), F32)], axis=0
     )
     t_scr[...] = stacked.T
-    for p in range(groups):
-        send_buf[p] = t_scr[pl.ds(p, per, stride=groups), :].astype(BF16)
 
     pl.semaphore_wait(barrier, groups - 1 + 2 * len(leaps))
 
     spread = []
     for d in range(1, groups):
         to = lax.rem(g + d, groups)
+        send_buf[to] = t_scr[pl.ds(to, per, stride=groups), :].astype(BF16)
         copy = pltpu.make_async_remote_copy(
             src_ref=send_buf.at[to],
             dst_ref=got.at[g],
@@ -80,7 +79,7 @@
         )
         copy.start()
         spread.append(copy)
-    got[g] = send_buf[g]
+    got[g] = t_scr[pl.ds(g, per, stride=groups), :].astype(BF16)
 
     main = rg.shape[1]
     loads[1].wait()

time: 62.7 us -> 62.7 us (level)
  no operation moved by 1% of the time
where the time goes in v7:
time: 62.7 us; the launch traced here: 62.5 us
  Pallas kernels  61.9 us (99%)
  local copies, waits for them, and re-layouts  0.63 us (1%)
    pallas_call x1, Pallas kernels, body(): pl.pallas_call(functools.partial(gather_kernel, groups, ring), out_shape=...  42.1 us
    pallas_call x1, Pallas kernels, body(): pl.pallas_call(scatter_kernel, out_shape=jax.ShapeDtypeStruct((1, rows, c...  16.8 us
    pallas_call x1, Pallas kernels, body(): pl.pallas_call(functools.partial(combine_kernel, 128), out_shape=(sums, s...  3.08 us

profile of v7, /device:TPU:1, one launch (start us, length us, event | category | flops | bytes accessed | tf_op | source)
XLA Modules:
  0.0 62.5 jit_solution(1401382694786082551)
XLA Ops:
  0.0 42.1 %gather_psi.1 = (f32[34,4,32,128]{3,2,1,0:T(8,128)S(1)}, bf16[640,512]{1,0:T(8,128)(2,1)S(1)}, s32[4,128]{1,0:T(4,128)S(1)}) custom-call(f32[1,32,512]{2,1,0:T(8,128)} %psi_hbm.1, bf16[34,32,512]{2,1,0:T(8,128)(2,1)} %left_hbm.1, bf16[34,32,512]{2,1,0:T(8,128)(2,1)} %right_hbm.1, s32[4,128]{1,0:T(4,128)} %bitcast.9, s32[4,128]{1,0:T(4,128)} %bitcast.10, ...), custom_call_target="tpu_custom_call" | custom-call | tf_op jit(solution)/shard_map/gather_psi/pallas_call | solution.py:392
  42.1 3.1 %combine_tasks.1 = (f32[160,4,8,128]{3,2,1,0:T(8,128)S(1)}, f32[160,4,8,128]{3,2,1,0:T(8,128)S(1)}) custom-call(f32[136,4,8,128]{3,2,1,0:T(8,128)S(1)} %bitcast.8, s32[4,128]{1,0:T(4,128)S(1)} %get-tuple-element.11.pk_ref), custom_call_target="tpu_custom_call" | custom-call | tf_op jit(solution)/shard_map/combine_tasks/pallas_call | solution.py:429
  45.1 16.8 %scatter_sums.1 = f32[1,32,512]{2,1,0:T(8,128)S(1)} custom-call(f32[16,2,5,32,128]{4,3,2,1,0:T(8,128)S(1)} %bitcast.6, f32[16,2,5,32,128]{4,3,2,1,0:T(8,128)S(1)} %bitcast.7, bf16[640,512]{1,0:T(8,128)(2,1)S(1)} %get-tuple-element.14.rt_ref), custom_call_target="tpu_custom_call" | custom-call | tf_op jit(solution)/shard_map/scatter_sums/pallas_call | solution.py:440
  61.9 0.6 %copy.8 = f32[1,32,512]{2,1,0:T(8,128)} copy(f32[1,32,512]{2,1,0:T(8,128)S(1)} %scatter_sums.1) | data formatting | bytes 131072
